TPU v7x, 32 devices: a whole 2x2x4 slice. The times are simulated.
32 devices in a mesh: section: 4 (over x, core), row: 8 (over z, y).
Axes of the slice: x: 2, y: 2, z: 4, core: 2. Of those that a mesh axis runs over, the one named last changes fastest.
Arguments:
- pair_in: bfloat16 [4, 256, 256, 128], P('section', 'row'), may hold values from -6 to 6
- upstream: bfloat16 [4, 256, 256, 128], P('section', 'row'), may hold values from -6 to 6
- chain_ids: int32 [256], replicated, may hold values from 0 to 2, never falling along the last dimension, each value on 1 to 192 neighbouring positions
- crop_mask: int32 [256], replicated, may hold values 0 or 1
- weight_in: bfloat16 [4, 2, 128, 640], P('section'), may hold values from -0.5 to 0.5
- weight_out: bfloat16 [4, 2, 128, 128], P('section'), may hold values from -0.5 to 0.5
- gain_in: float32 [4, 2, 128], P('section'), may hold values from 0.25 to 1.75
- bias_in: float32 [4, 2, 128], P('section'), may hold values from -3 to 3
- gain_out: float32 [4, 2, 128], P('section'), may hold values from 0.25 to 1.75
- bias_out: float32 [4, 2, 128], P('section'), may hold values from -3 to 3
Outputs:
- next_cotangent: bfloat16 [4, 256, 256, 128], P('section', 'row')
- grad_weight_in: float32 [4, 2, 128, 640], P('section')
- grad_weight_out: float32 [4, 2, 128, 128], P('section')
- grad_norm_in: float32 [4, 2, 2, 128], P('section')
- grad_norm_out: float32 [4, 2, 2, 128], P('section')
Inputs may be any that keep to these rules, and one draw needn't show every extreme that they name: `chain_ids`: chain numbers never fall along the residues; the longest chain holds 192 residues. `crop_mask`: 1 marks a residue present in the crop.
All inputs are finite; a program needn't handle non-finite values.
Results may differ from a plain program's by a relative error of at most 0.014.
Values may be sent and summed in bfloat16 or wider, within the bound.
A program may use at most 192 MiB of HBM per device.

v0:
```python
import jax
import jax.numpy as jnp
from jax import lax
from jax.sharding import PartitionSpec as P

epsilon = 1e-05


def passed_along(array, axis, by):
    length = lax.axis_size(axis)
    return lax.ppermute(array, axis, [(i, (i + by) % length) for i in range(length)])


def multiply(pattern, first_part, second):
    return jnp.einsum(pattern, first_part, second, preferred_element_type=jnp.float32)


def fold(array):
    quarter = array.shape[-1] // 4
    half = array.shape[0] // 2
    tail = array[..., 2 * quarter : 3 * quarter]
    zeros = jnp.zeros_like(tail)
    kept = array[..., : 2 * quarter] + jnp.concatenate([array[..., 3 * quarter :], zeros], axis=-1)
    return jnp.concatenate([kept[:half], kept[half:], tail[:half], tail[half:]], axis=-1)


def unfold(array, mask):
    quarter = array.shape[-1] // 6

    def one(kept, tail):
        return jnp.concatenate([kept, tail, kept[..., :quarter]], axis=-1)

    both = jnp.concatenate(
        [
            one(array[..., : 2 * quarter], array[..., 4 * quarter : 5 * quarter]),
            one(array[..., 2 * quarter : 4 * quarter], array[..., 5 * quarter :]),
        ],
        axis=0,
    )
    if mask is None:
        return both
    return jnp.where(mask, both, jnp.zeros_like(both))


def to_channels(array, mask):
    moved = lax.all_to_all(fold(array), "row", split_axis=0, concat_axis=1, tiled=True)
    return unfold(moved, mask)


def to_rows(array, mask):
    moved = lax.all_to_all(fold(array), "row", split_axis=1, concat_axis=0, tiled=True)
    return unfold(moved, mask)


def reduced(sums):
    weights_in, weights_out, norm_in, norm_out = sums
    norms = jnp.concatenate([norm_in, norm_out], axis=0)
    columns = weights_out.shape[1]
    norms = jnp.pad(norms, ((0, columns - norms.shape[0]), (0, 0))).T
    flat = jnp.concatenate([weights_in, weights_out, norms], axis=1).astype(jnp.bfloat16)
    width = lax.axis_size("row")
    parts = flat.reshape(width, flat.shape[0] // width, flat.shape[1])
    parts = lax.all_to_all(parts, "row", split_axis=0, concat_axis=0, tiled=True)
    summed = jnp.sum(parts.astype(jnp.float32), axis=0).astype(jnp.bfloat16)
    total = lax.all_gather(summed, "row", axis=0, tiled=True).astype(jnp.float32)
    split = weights_in.shape[1]
    norms = total[:, split + columns : split + columns + 4].T
    return (total[:, :split], total[:, split : split + columns], norms[:2], norms[2:])


def layer_inputs(pair_rows, pair_mask, weight_inner, gain_inner, bias_inner, hidden):
    values = pair_rows.astype(jnp.float32)
    centered = values - jnp.mean(values, axis=-1, keepdims=True)
    inverse_scale = lax.rsqrt(jnp.mean(centered * centered, axis=-1, keepdims=True) + epsilon)
    normal_in = centered * inverse_scale
    normed = (normal_in * gain_inner + bias_inner).astype(jnp.bfloat16)
    projected = multiply("rnc,cf->frn", normed, weight_inner[:, : 4 * hidden])
    gating = jax.nn.sigmoid(multiply("rnc,cf->rnf", normed, weight_inner[:, 4 * hidden :]))
    left_sigmoid = jax.nn.sigmoid(projected[:hidden])
    right_sigmoid = jax.nn.sigmoid(projected[2 * hidden : 3 * hidden])
    left_edges = (pair_mask * left_sigmoid * projected[hidden : 2 * hidden]).astype(jnp.bfloat16)
    right_edges = (pair_mask * right_sigmoid * projected[3 * hidden :]).astype(jnp.bfloat16)
    saved_in = (normal_in, inverse_scale, normed, projected, left_sigmoid, right_sigmoid, gating)
    return (left_edges, right_edges, saved_in)


def triangle_forward(left_edges, right_edges, outgoing):
    if outgoing:
        product = multiply("hik,hjk->hij", left_edges, right_edges)
    else:
        product = multiply("hki,hkj->hij", left_edges, right_edges)
    return product.astype(jnp.bfloat16)


def triangle_backward(grad_product, left_edges, right_edges, outgoing):
    if outgoing:
        grad_leftside = multiply("hij,hjk->hik", grad_product, right_edges)
        grad_rightside = multiply("hij,hik->hjk", grad_product, left_edges)
    else:
        grad_leftside = multiply("hij,hkj->hki", grad_product, right_edges)
        grad_rightside = multiply("hij,hki->hkj", grad_product, left_edges)
    return (grad_leftside.astype(jnp.bfloat16), grad_rightside.astype(jnp.bfloat16))


def layer_output(pair_rows, product, gating, gain_outer, bias_outer, weight_outer):
    values = product.astype(jnp.float32)
    centered = values - jnp.mean(values, axis=0, keepdims=True)
    inverse_scale = lax.rsqrt(jnp.mean(centered * centered, axis=0, keepdims=True) + epsilon)
    normal_out = centered * inverse_scale
    normed = (normal_out * gain_outer[:, None, None] + bias_outer[:, None, None]).astype(
        jnp.bfloat16
    )
    branch = multiply("hrn,hc->rnc", normed, weight_outer)
    updated = (pair_rows.astype(jnp.float32) + gating * branch).astype(jnp.bfloat16)
    return (updated, (normal_out, inverse_scale, normed, branch))


def output_backward(grad_pair, gating, saved_out, gain_outer, weight_outer):
    normal_out, inverse_scale, normed, branch = saved_out
    upstream_values = grad_pair.astype(jnp.float32)
    grad_branch = (upstream_values * gating).astype(jnp.bfloat16)
    grad_gate = (upstream_values * branch * gating * (1.0 - gating)).astype(jnp.bfloat16)
    grad_weight_out = multiply("hrn,rnc->hc", normed, grad_branch)
    grad_normed = multiply("rnc,hc->hrn", grad_branch, weight_outer)
    grad_gain = jnp.sum(grad_normed * normal_out, axis=(1, 2))
    grad_bias = jnp.sum(grad_normed, axis=(1, 2))
    scaled = grad_normed * gain_outer[:, None, None]
    grad_product = inverse_scale * (
        scaled
        - jnp.mean(scaled, axis=0, keepdims=True)
        - normal_out * jnp.mean(scaled * normal_out, axis=0, keepdims=True)
    )
    return (
        grad_product.astype(jnp.bfloat16),
        grad_gate,
        grad_weight_out,
        jnp.stack([grad_gain, grad_bias]),
    )


def input_backward(
    grad_leftside, grad_rightside, grad_gate, saved_in, pair_mask, weight_inner, gain_inner, hidden
):
    normal_in, inverse_scale, normed, projected, left_sigmoid, right_sigmoid, gating = saved_in
    left_values = grad_leftside.astype(jnp.float32) * pair_mask
    right_values = grad_rightside.astype(jnp.float32) * pair_mask
    grad_projected = jnp.concatenate(
        [
            left_values * projected[hidden : 2 * hidden] * left_sigmoid * (1.0 - left_sigmoid),
            left_values * left_sigmoid,
            right_values * projected[3 * hidden :] * right_sigmoid * (1.0 - right_sigmoid),
            right_values * right_sigmoid,
        ],
        axis=0,
    ).astype(jnp.bfloat16)
    grad_weight_in = jnp.concatenate(
        [
            multiply("rnc,frn->cf", normed, grad_projected),
            multiply("rnc,rnf->cf", normed, grad_gate),
        ],
        axis=1,
    )
    grad_normed = multiply("frn,cf->rnc", grad_projected, weight_inner[:, : 4 * hidden]) + multiply(
        "rnf,cf->rnc", grad_gate, weight_inner[:, 4 * hidden :]
    )
    grad_gain = jnp.sum(grad_normed * normal_in, axis=(0, 1))
    grad_bias = jnp.sum(grad_normed, axis=(0, 1))
    scaled = grad_normed * gain_inner
    grad_pair = inverse_scale * (
        scaled
        - jnp.mean(scaled, axis=-1, keepdims=True)
        - normal_in * jnp.mean(scaled * normal_in, axis=-1, keepdims=True)
    )
    return (grad_pair, grad_weight_in, jnp.stack([grad_gain, grad_bias]))


def per_device(
    pair_in,
    upstream,
    chain_ids,
    crop_mask,
    weight_in,
    weight_out,
    gain_in,
    bias_in,
    gain_out,
    bias_out,
):
    row_count = pair_in.shape[1]
    hidden = weight_out.shape[2]
    row_start = lax.axis_index("row") * row_count
    row_chain = lax.dynamic_slice_in_dim(chain_ids, row_start, row_count)
    row_crop = lax.dynamic_slice_in_dim(crop_mask, row_start, row_count)
    same_chain = row_chain[:, None] == chain_ids[None, :]
    pair_mask = jnp.where(same_chain, row_crop[:, None] * crop_mask[None, :], 0).astype(jnp.float32)
    row_mask = pair_mask > 0
    full_mask = (chain_ids[:, None] == chain_ids[None, :]) & (
        crop_mask[:, None] * crop_mask[None, :] > 0
    )
    pair_rows = pair_in[0]
    grad_top = upstream[0]

    def forward_update(source, direction, outgoing):
        left_edges, right_edges, saved_in = layer_inputs(
            source,
            pair_mask,
            weight_in[0, direction],
            gain_in[0, direction],
            bias_in[0, direction],
            hidden,
        )
        left_channels = to_channels(left_edges, full_mask)
        right_channels = to_channels(right_edges, full_mask)
        product = to_rows(triangle_forward(left_channels, right_channels, outgoing), row_mask)
        updated, saved_out = layer_output(
            source,
            product,
            saved_in[6],
            gain_out[0, direction],
            bias_out[0, direction],
            weight_out[0, direction],
        )
        return (updated, (left_channels, right_channels, saved_in, saved_out))

    def backward_update(grad_pair, stored, direction, outgoing):
        left_channels, right_channels, saved_in, saved_out = stored
        grad_product, grad_gate, grad_weight_out, grad_norm_out = output_backward(
            grad_pair, saved_in[6], saved_out, gain_out[0, direction], weight_out[0, direction]
        )
        grad_product = jnp.where(row_mask, grad_product, jnp.zeros_like(grad_product))
        grad_channels = to_channels(grad_product, full_mask)
        left_grads, right_grads = triangle_backward(
            grad_channels, left_channels, right_channels, outgoing
        )
        left_grads = jnp.where(full_mask, left_grads, jnp.zeros_like(left_grads))
        right_grads = jnp.where(full_mask, right_grads, jnp.zeros_like(right_grads))
        grad_leftside = to_rows(left_grads, None)
        grad_rightside = to_rows(right_grads, None)
        branch_grad, grad_weight_in, grad_norm_in = input_backward(
            grad_leftside,
            grad_rightside,
            grad_gate,
            saved_in,
            pair_mask,
            weight_in[0, direction],
            gain_in[0, direction],
            hidden,
        )
        return (branch_grad, (grad_weight_in, grad_weight_out, grad_norm_in, grad_norm_out))

    middle, stored_outgoing = forward_update(pair_rows, 0, True)
    top_unused, stored_incoming = forward_update(middle, 1, False)
    grad_inner, sums_incoming = backward_update(grad_top, stored_incoming, 1, False)
    grad_middle = (grad_top.astype(jnp.float32) + grad_inner).astype(jnp.bfloat16)
    grad_outer, sums_outgoing = backward_update(grad_middle, stored_outgoing, 0, True)
    outer_rounded = lax.optimization_barrier(grad_outer.astype(jnp.bfloat16))
    grad_input = (grad_middle.astype(jnp.float32) + outer_rounded.astype(jnp.float32)).astype(
        jnp.bfloat16
    )
    passed_back = passed_along(grad_input, "section", -1)
    incoming_totals = reduced(sums_incoming)
    outgoing_totals = reduced(sums_outgoing)
    totals = [jnp.stack([outgoing_totals[member], incoming_totals[member]]) for member in range(4)]
    inverse_n = 1.0 / pair_rows.shape[1]
    return (
        passed_back[None],
        totals[0][None] * inverse_n,
        totals[1][None] * inverse_n,
        totals[2][None] * inverse_n,
        totals[3][None] * inverse_n,
    )


def solution(mesh):
    return jax.shard_map(
        per_device,
        mesh=mesh,
        in_specs=(
            P("section", "row", None, None),
            P("section", "row", None, None),
            P(),
            P(),
            P("section", None, None, None),
            P("section", None, None, None),
            P("section", None, None),
            P("section", None, None),
            P("section", None, None),
            P("section", None, None),
        ),
        out_specs=(
            P("section", "row", None, None),
            P("section", None, None, None),
            P("section", None, None, None),
            P("section", None, None, None),
            P("section", None, None, None),
        ),
        check_vma=False,
    )
```

profile of v0, /device:TPU:0, one launch (start us, length us, event | category | flops | bytes accessed | tf_op | source)
XLA Modules:
  0.0 846.4 jit_solution(3344272591239111677)
XLA Ops:
  10.5 5.1 multiply_convert_fusion.11
  20.1 4.8 copy.473
  25.0 7.3 all-to-all-start.1
  38.8 4.8 copy.465
  43.7 25.7 %all-to-all-done.1 = bf16[64,32,384]{2,1,0:T(8,128)(2,1)} async-done(((bf16[64,32,384]{2,1,0:T(8,128)(2,1)}), bf16[64,32,384]{2,1,0:T(8,128)(2,1)}, u32[]{:S(2)}, u32[]{:S(2)}) %all-to-all-start.1) | async-done | bytes 1572896 | tf_op jit(solution)/shard_map/all_to_all | solution.py:46
  69.3 4.6 all-to-all-start
  77.7 32.8 %all-to-all-done = bf16[64,32,384]{2,1,0:T(8,128)(2,1)} async-done(((bf16[64,32,384]{2,1,0:T(8,128)(2,1)}), bf16[64,32,384]{2,1,0:T(8,128)(2,1)}, u32[]{:S(2)}, u32[]{:S(2)}) %all-to-all-start) | async-done | bytes 1572896 | tf_op jit(solution)/shard_map/all_to_all | solution.py:46
  141.1 4.8 all-to-all-start.2
  146.6 36.0 %all-to-all-done.2 = bf16[8,256,384]{2,0,1:T(8,128)(2,1)} async-done(((bf16[8,256,384]{2,0,1:T(8,128)(2,1)}), bf16[8,256,384]{2,0,1:T(8,128)(2,1)}, u32[]{:S(2)}, u32[]{:S(2)}) %all-to-all-start.2) | async-done | bytes 1572896 | tf_op jit(solution)/shard_map/all_to_all | solution.py:51
  189.3 4.6 convert_reduce_fusion.1
  197.7 5.0 multiply_convert_fusion.9
  209.3 4.6 all-to-all-start.4
  219.9 30.6 %all-to-all-done.4 = bf16[64,32,384]{2,1,0:T(8,128)(2,1)} async-done(((bf16[64,32,384]{2,1,0:T(8,128)(2,1)}), bf16[64,32,384]{2,1,0:T(8,128)(2,1)}, u32[]{:S(2)}, u32[]{:S(2)}) %all-to-all-start.4) | async-done | bytes 1572896 | tf_op jit(solution)/shard_map/all_to_all | solution.py:46
  257.7 33.7 %all-to-all-done.3 = bf16[64,32,384]{2,1,0:T(8,128)(2,1)S(1)} async-done(((bf16[64,32,384]{2,1,0:T(8,128)(2,1)}), bf16[64,32,384]{2,1,0:T(8,128)(2,1)S(1)}, u32[]{:S(2)}, u32[]{:S(2)}) %all-to-all-start.3) | async-done | bytes 1572896 | tf_op jit(solution)/shard_map/all_to_all | solution.py:46
  310.6 4.8 all-to-all-start.5
  323.4 28.7 %all-to-all-done.5 = bf16[8,256,384]{2,0,1:T(8,128)(2,1)} async-done(((bf16[8,256,384]{2,0,1:T(8,128)(2,1)}), bf16[8,256,384]{2,0,1:T(8,128)(2,1)}, u32[]{:S(2)}, u32[]{:S(2)}) %all-to-all-start.5) | async-done | bytes 1572896 | tf_op jit(solution)/shard_map/all_to_all | solution.py:51
  364.8 40.7 %all_to_all.226 = bf16[64,32,384]{2,1,0:T(8,128)(2,1)S(1)} all-to-all(bf16[64,32,384]{2,1,0:T(8,128)(2,1)S(1)} %copy.511), channel_id=1, replica_groups=mesh['section'=4,'row'=8] {'row'}, dimensions={0} | all-to-all | bytes 3145728 | tf_op jit(solution)/shard_map/all_to_all | solution.py:46
  435.5 28.7 %all-to-all-done.8 = bf16[8,256,384]{2,0,1:T(8,128)(2,1)} async-done(((bf16[8,256,384]{2,0,1:T(8,128)(2,1)}), bf16[8,256,384]{2,0,1:T(8,128)(2,1)}, u32[]{:S(2)}, u32[]{:S(2)}) %all-to-all-start.8) | async-done | bytes 1572896 | tf_op jit(solution)/shard_map/all_to_all | solution.py:51
  468.5 6.0 fusion.68
  479.0 26.0 %all-to-all-done.7 = bf16[8,256,384]{2,0,1:T(8,128)(2,1)} async-done(((bf16[8,256,384]{2,0,1:T(8,128)(2,1)}), bf16[8,256,384]{2,0,1:T(8,128)(2,1)}, u32[]{:S(2)}, u32[]{:S(2)}) %all-to-all-start.7) | async-done | bytes 1572896 | tf_op jit(solution)/shard_map/all_to_all | solution.py:51
  538.0 6.6 multiply_convert_fusion.5
  544.7 7.6 multiply_convert_fusion.7
  574.2 4.6 all-to-all-start.9
  586.9 4.8 fusion.98
  592.4 23.0 %all-to-all-done.9 = bf16[64,32,384]{2,1,0:T(8,128)(2,1)} async-done(((bf16[64,32,384]{2,1,0:T(8,128)(2,1)}), bf16[64,32,384]{2,1,0:T(8,128)(2,1)}, u32[]{:S(2)}, u32[]{:S(2)}) %all-to-all-start.9) | async-done | bytes 1572896 | tf_op jit(solution)/shard_map/all_to_all | solution.py:46
  629.5 6.0 all-to-all-start.11
  642.6 29.7 %all-to-all-done.11 = bf16[8,256,384]{2,0,1:T(8,128)(2,1)} async-done(((bf16[8,256,384]{2,0,1:T(8,128)(2,1)}), bf16[8,256,384]{2,0,1:T(8,128)(2,1)}, u32[]{:S(2)}, u32[]{:S(2)}) %all-to-all-start.11) | async-done | bytes 1572896 | tf_op jit(solution)/shard_map/all_to_all | solution.py:51
  689.5 44.1 %all_gather.7 = bf16[128,896]{1,0:T(8,128)(2,1)S(1)} all-gather(bf16[16,896]{1,0:T(8,128)(2,1)S(1)} %reduce_sum.265), channel_id=1, replica_groups=mesh['section'=4,'row'=8] {'row'}, dimensions={0}, use_global_device_ids=true | all-gather | bytes 258048 | tf_op jit(solution)/shard_map/all_gather | solution.py:65
  772.4 6.7 multiply_convert_fusion.1
  779.2 5.8 multiply_convert_fusion.3
  799.0 9.0 %all-to-all-done.12 = bf16[8,16,896]{2,1,0:T(8,128)(2,1)S(1)} async-done(((bf16[8,16,896]{2,1,0:T(8,128)(2,1)}), bf16[8,16,896]{2,1,0:T(8,128)(2,1)S(1)}, u32[]{:S(2)}, u32[]{:S(2)}) %all-to-all-start.12) | async-done | bytes 229408 | tf_op jit(solution)/shard_map/all_to_all | solution.py:63
  808.0 30.8 %all_gather.6 = bf16[128,896]{1,0:T(8,128)(2,1)S(1)} all-gather(bf16[16,896]{1,0:T(8,128)(2,1)S(1)} %reduce_sum.260), channel_id=1, replica_groups=mesh['section'=4,'row'=8] {'row'}, dimensions={0}, use_global_device_ids=true | all-gather | bytes 258048 | tf_op jit(solution)/shard_map/all_gather | solution.py:65
  (492 shorter events, 324.6 us)
Async XLA Ops:
  6.7 182.4 %copy-start.2 = (bf16[1,32,256,128]{2,3,1,0:T(8,128)(2,1)}, bf16[1,32,256,128]{2,3,1,0:T(8,128)(2,1)S(1)}, u32[]{:S(2)}) copy-start(bf16[1,32,256,128]{2,3,1,0:T(8,128)(2,1)S(1)} %copy.460) | copy-start | bytes 6291460
  7.1 182.1 %copy-start.50 = (f32[32,256]{1,0:T(8,128)}, f32[32,256]{1,0:T(8,128)S(1)}, u32[]{:S(2)}) copy-start(f32[32,256]{1,0:T(8,128)S(1)} %broadcast_multiply_fusion.11) | copy-start | bytes 98308
  7.9 181.3 %copy-start.54 = (f32[32,256]{1,0:T(8,128)}, f32[32,256]{1,0:T(8,128)S(1)}, u32[]{:S(2)}) copy-start(f32[32,256]{1,0:T(8,128)S(1)} %add_rsqrt_fusion.3) | copy-start | bytes 98308
  7.9 181.3 %copy-start.91 = (f32[128]{0:T(128)}, f32[128]{0:T(128)S(1)}, u32[]{:S(2)}) copy-start(f32[128]{0:T(128)S(1)} %get-tuple-element.203) | copy-start | bytes 1540
  7.9 181.3 %copy-start.97 = (f32[128]{0:T(128)}, f32[128]{0:T(128)S(1)}, u32[]{:S(2)}) copy-start(f32[128]{0:T(128)S(1)} %get-tuple-element.197) | copy-start | bytes 1540
  7.9 311.6 %copy-start.101 = (f32[128]{0:T(128)}, f32[128]{0:T(128)S(1)}, u32[]{:S(2)}) copy-start(f32[128]{0:T(128)S(1)} %get-tuple-element.196) | copy-start | bytes 1540
  25.0 44.4 %all-to-all-start.1 = ((bf16[64,32,384]{2,1,0:T(8,128)(2,1)}), bf16[64,32,384]{2,1,0:T(8,128)(2,1)}, u32[]{:S(2)}, u32[]{:S(2)}) async-start(bf16[64,32,384]{2,1,0:T(8,128)(2,1)} %copy.473), calls=%async_computation.1 | async-start | bytes 3145728 | tf_op jit(solution)/shard_map/all_to_all | solution.py:46
  69.3 41.2 %all-to-all-start = ((bf16[64,32,384]{2,1,0:T(8,128)(2,1)}), bf16[64,32,384]{2,1,0:T(8,128)(2,1)}, u32[]{:S(2)}, u32[]{:S(2)}) async-start(bf16[64,32,384]{2,1,0:T(8,128)(2,1)} %copy.465), calls=%async_computation | async-start | bytes 3145728 | tf_op jit(solution)/shard_map/all_to_all | solution.py:46
  74.1 59.5 %copy-start.87 = (pred[256,256]{0,1:T(8,128)(4,1)}, pred[256,256]{0,1:T(8,128)(4,1)S(1)}, u32[]{:S(2)}) copy-start(pred[256,256]{0,1:T(8,128)(4,1)S(1)} %fusion.108) | copy-start | bytes 196612
  117.3 15.4 %copy-start.41 = (bf16[8,256,64]{2,1,0:T(8,128)(2,1)S(1)}, bf16[8,256,64]{2,1,0:T(8,128)(2,1)}, u32[]{:S(2)}) copy-start(bf16[8,256,64]{2,1,0:T(8,128)(2,1)} %get-tuple-element.153) | copy-start | bytes 786436
  141.1 41.4 %all-to-all-start.2 = ((bf16[8,256,384]{2,0,1:T(8,128)(2,1)}), bf16[8,256,384]{2,0,1:T(8,128)(2,1)}, u32[]{:S(2)}, u32[]{:S(2)}) async-start(bf16[8,256,384]{2,0,1:T(8,128)(2,1)} %copy.483), calls=%async_computation.2 | async-start | bytes 3145728 | tf_op jit(solution)/shard_map/all_to_all | solution.py:51
  146.5 41.1 %copy-start.93 = (f32[128]{0:T(128)}, f32[128]{0:T(128)S(1)}, u32[]{:S(2)}) copy-start(f32[128]{0:T(128)S(1)} %get-tuple-element.205) | copy-start | bytes 1540
  146.5 41.1 %copy-start.99 = (f32[128]{0:T(128)}, f32[128]{0:T(128)S(1)}, u32[]{:S(2)}) copy-start(f32[128]{0:T(128)S(1)} %get-tuple-element.191) | copy-start | bytes 1540
  146.5 322.0 %copy-start.95 = (f32[128]{0:T(128)}, f32[128]{0:T(128)S(1)}, u32[]{:S(2)}) copy-start(f32[128]{0:T(128)S(1)} %get-tuple-element.206) | copy-start | bytes 1540
  209.3 41.2 %all-to-all-start.4 = ((bf16[64,32,384]{2,1,0:T(8,128)(2,1)}), bf16[64,32,384]{2,1,0:T(8,128)(2,1)}, u32[]{:S(2)}, u32[]{:S(2)}) async-start(bf16[64,32,384]{2,1,0:T(8,128)(2,1)} %copy.496), calls=%async_computation.4 | async-start | bytes 3145728 | tf_op jit(solution)/shard_map/all_to_all | solution.py:46
  250.5 40.8 %all-to-all-start.3 = ((bf16[64,32,384]{2,1,0:T(8,128)(2,1)}), bf16[64,32,384]{2,1,0:T(8,128)(2,1)S(1)}, u32[]{:S(2)}, u32[]{:S(2)}) async-start(bf16[64,32,384]{2,1,0:T(8,128)(2,1)} %copy.488), calls=%async_computation.3 | async-start | bytes 3145728 | tf_op jit(solution)/shard_map/all_to_all | solution.py:46
  310.6 41.5 %all-to-all-start.5 = ((bf16[8,256,384]{2,0,1:T(8,128)(2,1)}), bf16[8,256,384]{2,0,1:T(8,128)(2,1)}, u32[]{:S(2)}, u32[]{:S(2)}) async-start(bf16[8,256,384]{2,0,1:T(8,128)(2,1)} %copy.505), calls=%async_computation.5 | async-start | bytes 3145728 | tf_op jit(solution)/shard_map/all_to_all | solution.py:51
  423.7 40.5 %all-to-all-start.8 = ((bf16[8,256,384]{2,0,1:T(8,128)(2,1)}), bf16[8,256,384]{2,0,1:T(8,128)(2,1)}, u32[]{:S(2)}, u32[]{:S(2)}) async-start(bf16[8,256,384]{2,0,1:T(8,128)(2,1)} %copy.531), calls=%async_computation.8 | async-start | bytes 3145728 | tf_op jit(solution)/shard_map/all_to_all | solution.py:51
  431.3 37.2 %copy-start.83 = (bf16[1,2,128,128]{3,2,1,0:T(8,128)(2,1)S(1)}, bf16[1,2,128,128]{3,2,1,0:T(8,128)(2,1)}, u32[]{:S(2)}) copy-start(bf16[1,2,128,128]{3,2,1,0:T(8,128)(2,1)} %param.15) | copy-start | bytes 196612
  431.3 37.2 %copy-start.107 = (f32[128]{0:T(128)S(1)}, f32[128]{0:T(128)}, u32[]{:S(2)}) copy-start(f32[128]{0:T(128)} %get-tuple-element.190) | copy-start | bytes 1540
  464.2 40.8 %all-to-all-start.7 = ((bf16[8,256,384]{2,0,1:T(8,128)(2,1)}), bf16[8,256,384]{2,0,1:T(8,128)(2,1)}, u32[]{:S(2)}, u32[]{:S(2)}) async-start(bf16[8,256,384]{2,0,1:T(8,128)(2,1)} %copy.521), calls=%async_computation.7 | async-start | bytes 3145728 | tf_op jit(solution)/shard_map/all_to_all | solution.py:51
  574.2 41.2 %all-to-all-start.9 = ((bf16[64,32,384]{2,1,0:T(8,128)(2,1)}), bf16[64,32,384]{2,1,0:T(8,128)(2,1)}, u32[]{:S(2)}, u32[]{:S(2)}) async-start(bf16[64,32,384]{2,1,0:T(8,128)(2,1)} %copy.547), calls=%async_computation.9 | async-start | bytes 3145728 | tf_op jit(solution)/shard_map/all_to_all | solution.py:46
  615.4 14.1 %all-to-all-start.13 = ((bf16[8,16,896]{2,1,0:T(8,128)(2,1)}), bf16[8,16,896]{2,1,0:T(8,128)(2,1)S(1)}, u32[]{:S(2)}, u32[]{:S(2)}) async-start(bf16[8,16,896]{2,1,0:T(8,128)(2,1)} %pad_maximum_fusion.23), calls=%async_computation.13 | async-start | bytes 458752 | tf_op jit(solution)/shard_map/all_to_all | solution.py:63
  629.5 42.7 %all-to-all-start.11 = ((bf16[8,256,384]{2,0,1:T(8,128)(2,1)}), bf16[8,256,384]{2,0,1:T(8,128)(2,1)}, u32[]{:S(2)}, u32[]{:S(2)}) async-start(bf16[8,256,384]{2,0,1:T(8,128)(2,1)} %copy.566), calls=%async_computation.11 | async-start | bytes 3145728 | tf_op jit(solution)/shard_map/all_to_all | solution.py:51
  638.4 38.4 %copy-start.3 = (bf16[1,32,256,128]{2,3,1,0:T(8,128)(2,1)S(1)}, bf16[1,32,256,128]{2,3,1,0:T(8,128)(2,1)}, u32[]{:S(2)}) copy-start(bf16[1,32,256,128]{2,3,1,0:T(8,128)(2,1)} %copy-done.2) | copy-start | bytes 6291460
  638.4 38.4 %copy-start.51 = (f32[32,256]{1,0:T(8,128)S(1)}, f32[32,256]{1,0:T(8,128)}, u32[]{:S(2)}) copy-start(f32[32,256]{1,0:T(8,128)} %copy-done.50) | copy-start | bytes 98308
  638.4 38.4 %copy-start.55 = (f32[32,256]{1,0:T(8,128)S(1)}, f32[32,256]{1,0:T(8,128)}, u32[]{:S(2)}) copy-start(f32[32,256]{1,0:T(8,128)} %copy-done.54) | copy-start | bytes 98308
  638.4 38.4 %copy-start.92 = (f32[128]{0:T(128)S(1)}, f32[128]{0:T(128)}, u32[]{:S(2)}) copy-start(f32[128]{0:T(128)} %copy-done.91) | copy-start | bytes 1540
  638.4 38.4 %copy-start.98 = (f32[128]{0:T(128)S(1)}, f32[128]{0:T(128)}, u32[]{:S(2)}) copy-start(f32[128]{0:T(128)} %copy-done.97) | copy-start | bytes 1540
  672.3 66.9 %all-to-all-start.10 = ((bf16[8,256,384]{2,0,1:T(8,128)(2,1)}), bf16[8,256,384]{2,0,1:T(8,128)(2,1)}, u32[]{:S(2)}, u32[]{:S(2)}) async-start(bf16[8,256,384]{2,0,1:T(8,128)(2,1)} %copy.556), calls=%async_computation.10 | async-start | bytes 3145728 | tf_op jit(solution)/shard_map/all_to_all | solution.py:51
  794.2 47.7 %collective-permute-start = (bf16[32,256,128]{1,2,0:T(8,128)(2,1)S(1)}, bf16[32,256,128]{1,2,0:T(8,128)(2,1)}, u32[]{:S(2)}, u32[]{:S(2)}) collective-permute-start(bf16[32,256,128]{1,2,0:T(8,128)(2,1)S(1)} %fusion.64), channel_id=1, source_target_pairs={{0,24},{8,0},{16,8},{24,16},{1,25},{9,1},{17,9},{25,17},{2,26},{10... | collective-permute-start | bytes 6291464 | tf_op jit(solution)/shard_map/ppermute | solution.py:11
  795.1 12.9 %all-to-all-start.12 = ((bf16[8,16,896]{2,1,0:T(8,128)(2,1)}), bf16[8,16,896]{2,1,0:T(8,128)(2,1)S(1)}, u32[]{:S(2)}, u32[]{:S(2)}) async-start(bf16[8,16,896]{2,1,0:T(8,128)(2,1)} %pad_maximum_fusion.22), calls=%async_computation.12 | async-start | bytes 458752 | tf_op jit(solution)/shard_map/all_to_all | solution.py:63
  (95 other events, 477.2 us)
where the time goes:
time: 857 us; the launch traced here: 846 us
  waiting for transfers between devices  304 us (35%)
  local copies, waits for them, and re-layouts  210 us (25%)
  blocking collectives  116 us (14%)
  other arithmetic  82.6 us (10%)
  matrix products  70 us (8%)
  starting transfers between devices  60.9 us (7%)
    all_to_all x6, waiting for transfers between devices, to_rows(): lax.all_to_all(fold(array), 'row', split_axis=1, concat_axis=0, tiled=True)  149 us
    all_to_all x5, waiting for transfers between devices, to_channels(): lax.all_to_all(fold(array), 'row', split_axis=0, concat_axis=1, tiled=True)  146 us
    unnamed x290, local copies, waits for them, and re-layouts  121 us
    all_gather x2, blocking collectives, reduced(): lax.all_gather(summed, 'row', axis=0, tiled=True).astype(jnp.float32)  74.9 us
    dot_general x24, matrix products, multiply(): jnp.einsum(pattern, first_part, second, preferred_element_type=jnp.float32)  70 us
    all_to_all x1, blocking collectives, to_channels(): lax.all_to_all(fold(array), 'row', split_axis=0, concat_axis=1, tiled=True)  40.7 us
    concatenate x12, local copies, waits for them, and re-layouts, fold(): jnp.concatenate([kept[:half], kept[half:], tail[:half], tail[half:]], axi...  35 us
    all_to_all x6, starting transfers between devices, to_rows(): lax.all_to_all(fold(array), 'row', split_axis=1, concat_axis=0, tiled=True)  28.7 us
  transfers between devices with their start and end apart: 14, of which 11 were waited for; matrix products, arithmetic and copies ran while one was open for 12% of the time, Pallas kernels for 0%

commit v1 on v0

--- a/solution.py
+++ b/solution.py
@@ -48,7 +48,12 @@
 
 
 def to_rows(array, mask):
-    moved = lax.all_to_all(fold(array), "row", split_axis=1, concat_axis=0, tiled=True)
+    moved = jnp.concatenate(
+        lax.all_to_all(
+            jnp.stack(jnp.split(fold(array), lax.axis_size("row"), axis=1)), "row", 0, 0
+        ),
+        axis=0,
+    )
     return unfold(moved, mask)
 
 

time: 857 us -> 952 us (1.11)
  local copies, waits for them, and re-layouts: 210 us -> 352 us
  waiting for transfers between devices: 304 us -> 258 us
    another operation x0 -> x60, local copies, waits for them, and re-layouts: none -> 99.5 us  [to_rows(): jnp.stack(jnp.split(fold(array), lax.axis_size('row'), axis=1))]
    unnamed x290 -> x362, local copies, waits for them, and re-layouts: 121 us -> 175 us
    all_to_all x6, waiting for transfers between devices: 149 us -> 102 us  [to_rows(): lax.all_to_all(jnp.stack(jnp.split(fold(array), lax.axis_size('row'), axi...]
    concatenate x12 -> x6, local copies, waits for them, and re-layouts: 35 us -> 19.2 us  [fold(): jnp.concatenate([kept[:half], kept[half:], tail[:half], tail[half:]], axi...]
  transfers between devices with their start and end apart: 14 -> 14, of which waited for: 11 -> 11; matrix products, arithmetic and copies ran while one was open for 12% -> 18% of each run, Pallas kernels for 0% -> 0%
where the time goes in v1:
time: 952 us; the launch traced here: 939 us
  local copies, waits for them, and re-layouts  352 us (37%)
  waiting for transfers between devices  258 us (27%)
  blocking collectives  116 us (12%)
  other arithmetic  77.3 us (8%)
  matrix products  71 us (7%)
  starting transfers between devices  61.3 us (6%)
    unnamed x362, local copies, waits for them, and re-layouts  175 us
    all_to_all x5, waiting for transfers between devices, to_channels(): lax.all_to_all(fold(array), 'row', split_axis=0, concat_axis=1, tiled=True)  147 us
    all_to_all x6, waiting for transfers between devices, to_rows(): lax.all_to_all(jnp.stack(jnp.split(fold(array), lax.axis_size('row'), axi...  102 us
    another operation x60, local copies, waits for them, and re-layouts, to_rows(): jnp.stack(jnp.split(fold(array), lax.axis_size('row'), axis=1))  99.5 us
    all_gather x2, blocking collectives, reduced(): lax.all_gather(summed, 'row', axis=0, tiled=True).astype(jnp.float32)  74.9 us
    dot_general x24, matrix products, multiply(): jnp.einsum(pattern, first_part, second, preferred_element_type=jnp.float32)  71 us
    all_to_all x1, blocking collectives, to_channels(): lax.all_to_all(fold(array), 'row', split_axis=0, concat_axis=1, tiled=True)  40.8 us
    all_to_all x6, starting transfers between devices, to_rows(): lax.all_to_all(jnp.stack(jnp.split(fold(array), lax.axis_size('row'), axi...  29 us
  transfers between devices with their start and end apart: 14, of which 11 were waited for; matrix products, arithmetic and copies ran while one was open for 18% of the time, Pallas kernels for 0%

profile of v1, /device:TPU:0, one launch (start us, length us, event | category | flops | bytes accessed | tf_op | source)
XLA Modules:
  0.0 939.2 jit_solution(6094539504073661520)
XLA Ops:
  11.6 5.1 multiply_convert_fusion.11
  21.2 4.9 copy.551
  26.1 7.3 all-to-all-start.1
  39.0 4.8 copy.543
  43.8 26.7 %all-to-all-done.1 = bf16[64,32,384]{2,1,0:T(8,128)(2,1)} async-done(((bf16[64,32,384]{2,1,0:T(8,128)(2,1)}), bf16[64,32,384]{2,1,0:T(8,128)(2,1)}, u32[]{:S(2)}, u32[]{:S(2)}) %all-to-all-start.1) | async-done | bytes 1572896 | tf_op jit(solution)/shard_map/all_to_all | solution.py:46
  79.4 32.2 %all-to-all-done = bf16[64,32,384]{2,1,0:T(8,128)(2,1)} async-done(((bf16[64,32,384]{2,1,0:T(8,128)(2,1)}), bf16[64,32,384]{2,1,0:T(8,128)(2,1)}, u32[]{:S(2)}, u32[]{:S(2)}) %all-to-all-start) | async-done | bytes 1572896 | tf_op jit(solution)/shard_map/all_to_all | solution.py:46
  166.7 4.5 all-to-all-start.2
  171.8 36.0 %all-to-all-done.2 = bf16[8,8,32,384]{3,2,1,0:T(8,128)(2,1)} async-done(((bf16[8,8,32,384]{3,2,1,0:T(8,128)(2,1)}), bf16[8,8,32,384]{3,2,1,0:T(8,128)(2,1)}, u32[]{:S(2)}, u32[]{:S(2)}) %all-to-all-start.2) | async-done | bytes 1572896 | tf_op jit(solution)/shard_map/all_to_all | solution.py:52
  214.9 4.9 convert_reduce_fusion.1
  223.7 5.1 multiply_convert_fusion.9
  235.2 4.8 all-to-all-start.4
  245.1 31.5 %all-to-all-done.4 = bf16[64,32,384]{2,1,0:T(8,128)(2,1)} async-done(((bf16[64,32,384]{2,1,0:T(8,128)(2,1)}), bf16[64,32,384]{2,1,0:T(8,128)(2,1)}, u32[]{:S(2)}, u32[]{:S(2)}) %all-to-all-start.4) | async-done | bytes 1572896 | tf_op jit(solution)/shard_map/all_to_all | solution.py:46
  283.7 33.7 %all-to-all-done.3 = bf16[64,32,384]{2,1,0:T(8,128)(2,1)S(1)} async-done(((bf16[64,32,384]{2,1,0:T(8,128)(2,1)}), bf16[64,32,384]{2,1,0:T(8,128)(2,1)S(1)}, u32[]{:S(2)}, u32[]{:S(2)}) %all-to-all-start.3) | async-done | bytes 1572896 | tf_op jit(solution)/shard_map/all_to_all | solution.py:46
  353.2 4.6 all-to-all-start.5
  362.0 4.5 add_divide_fusion
  366.4 28.0 %all-to-all-done.5 = bf16[8,8,32,384]{3,2,1,0:T(8,128)(2,1)} async-done(((bf16[8,8,32,384]{3,2,1,0:T(8,128)(2,1)}), bf16[8,8,32,384]{3,2,1,0:T(8,128)(2,1)}, u32[]{:S(2)}, u32[]{:S(2)}) %all-to-all-start.5) | async-done | bytes 1572896 | tf_op jit(solution)/shard_map/all_to_all | solution.py:52
  407.5 40.8 %all_to_all.148 = bf16[64,32,384]{2,1,0:T(8,128)(2,1)S(1)} all-to-all(bf16[64,32,384]{2,1,0:T(8,128)(2,1)S(1)} %copy.601), channel_id=1, replica_groups=mesh['section'=4,'row'=8] {'row'}, dimensions={0} | all-to-all | bytes 3145728 | tf_op jit(solution)/shard_map/all_to_all | solution.py:46
  532.4 4.7 all-to-all-start.7
  537.1 6.0 fusion.68
  548.5 24.7 %all-to-all-done.7 = bf16[8,8,32,384]{3,2,1,0:T(8,128)(2,1)} async-done(((bf16[8,8,32,384]{3,2,1,0:T(8,128)(2,1)}), bf16[8,8,32,384]{3,2,1,0:T(8,128)(2,1)}, u32[]{:S(2)}, u32[]{:S(2)}) %all-to-all-start.7) | async-done | bytes 1572896 | tf_op jit(solution)/shard_map/all_to_all | solution.py:52
  607.3 6.6 multiply_convert_fusion.5
  614.0 7.4 multiply_convert_fusion.7
  643.2 4.6 all-to-all-start.9
  655.9 4.8 fusion.98
  661.4 22.8 %all-to-all-done.9 = bf16[64,32,384]{2,1,0:T(8,128)(2,1)} async-done(((bf16[64,32,384]{2,1,0:T(8,128)(2,1)}), bf16[64,32,384]{2,1,0:T(8,128)(2,1)}, u32[]{:S(2)}, u32[]{:S(2)}) %all-to-all-start.9) | async-done | bytes 1572896 | tf_op jit(solution)/shard_map/all_to_all | solution.py:46
  720.4 6.5 all-to-all-start.11
  753.5 10.0 %all-to-all-done.11 = bf16[8,8,32,384]{3,2,1,0:T(8,128)(2,1)} async-done(((bf16[8,8,32,384]{3,2,1,0:T(8,128)(2,1)}), bf16[8,8,32,384]{3,2,1,0:T(8,128)(2,1)}, u32[]{:S(2)}, u32[]{:S(2)}) %all-to-all-start.11) | async-done | bytes 1572896 | tf_op jit(solution)/shard_map/all_to_all | solution.py:52
  780.6 44.1 %all_gather.7 = bf16[128,896]{1,0:T(8,128)(2,1)S(1)} all-gather(bf16[16,896]{1,0:T(8,128)(2,1)S(1)} %reduce_sum.265), channel_id=1, replica_groups=mesh['section'=4,'row'=8] {'row'}, dimensions={0}, use_global_device_ids=true | all-gather | bytes 258048 | tf_op jit(solution)/shard_map/all_gather | solution.py:70
  865.5 6.7 multiply_convert_fusion.1
  872.3 5.8 multiply_convert_fusion.3
  892.0 9.0 all-to-all-done.12
  901.1 30.8 %all_gather.6 = bf16[128,896]{1,0:T(8,128)(2,1)S(1)} all-gather(bf16[16,896]{1,0:T(8,128)(2,1)S(1)} %reduce_sum.260), channel_id=1, replica_groups=mesh['section'=4,'row'=8] {'row'}, dimensions={0}, use_global_device_ids=true | all-gather | bytes 258048 | tf_op jit(solution)/shard_map/all_gather | solution.py:70
  (614 shorter events, 461.7 us)
Async XLA Ops:
  7.3 207.5 %copy-start.2 = (bf16[1,32,256,128]{2,3,1,0:T(8,128)(2,1)}, bf16[1,32,256,128]{2,3,1,0:T(8,128)(2,1)S(1)}, u32[]{:S(2)}) copy-start(bf16[1,32,256,128]{2,3,1,0:T(8,128)(2,1)S(1)} %copy.538) | copy-start | bytes 6291460
  7.8 207.0 %copy-start.54 = (f32[32,256]{1,0:T(8,128)}, f32[32,256]{1,0:T(8,128)S(1)}, u32[]{:S(2)}) copy-start(f32[32,256]{1,0:T(8,128)S(1)} %broadcast_multiply_fusion.11) | copy-start | bytes 98308
  8.5 206.3 %copy-start.58 = (f32[32,256]{1,0:T(8,128)}, f32[32,256]{1,0:T(8,128)S(1)}, u32[]{:S(2)}) copy-start(f32[32,256]{1,0:T(8,128)S(1)} %add_rsqrt_fusion.3) | copy-start | bytes 98308
  9.0 205.8 %copy-start.107 = (f32[128]{0:T(128)}, f32[128]{0:T(128)S(1)}, u32[]{:S(2)}) copy-start(f32[128]{0:T(128)S(1)} %get-tuple-element.251) | copy-start | bytes 1540
  9.0 205.8 %copy-start.113 = (f32[128]{0:T(128)}, f32[128]{0:T(128)S(1)}, u32[]{:S(2)}) copy-start(f32[128]{0:T(128)S(1)} %get-tuple-element.245) | copy-start | bytes 1540
  26.1 44.4 %all-to-all-start.1 = ((bf16[64,32,384]{2,1,0:T(8,128)(2,1)}), bf16[64,32,384]{2,1,0:T(8,128)(2,1)}, u32[]{:S(2)}, u32[]{:S(2)}) async-start(bf16[64,32,384]{2,1,0:T(8,128)(2,1)} %copy.551), calls=%async_computation.1 | async-start | bytes 3145728 | tf_op jit(solution)/shard_map/all_to_all | solution.py:46
  70.5 41.1 %all-to-all-start = ((bf16[64,32,384]{2,1,0:T(8,128)(2,1)}), bf16[64,32,384]{2,1,0:T(8,128)(2,1)}, u32[]{:S(2)}, u32[]{:S(2)}) async-start(bf16[64,32,384]{2,1,0:T(8,128)(2,1)} %copy.543), calls=%async_computation | async-start | bytes 3145728 | tf_op jit(solution)/shard_map/all_to_all | solution.py:46
  155.5 15.7 %copy-start.127 = (f32[1,2,128]{2,1,0:T(2,128)S(1)}, f32[1,2,128]{2,1,0:T(2,128)}, u32[]{:S(2)}) copy-start(f32[1,2,128]{2,1,0:T(2,128)} %param.18) | copy-start | bytes 3076
  166.7 41.1 %all-to-all-start.2 = ((bf16[8,8,32,384]{3,2,1,0:T(8,128)(2,1)}), bf16[8,8,32,384]{3,2,1,0:T(8,128)(2,1)}, u32[]{:S(2)}, u32[]{:S(2)}) async-start(bf16[8,8,32,384]{3,2,1,0:T(8,128)(2,1)} %constant_dynamic-update-slice_fusion), calls=%async_computation.2 | async-start | bytes 3145728 | tf_op jit(solution)/shard_map/all_to_all | solution.py:52
  171.7 41.4 %copy-start.109 = (f32[128]{0:T(128)}, f32[128]{0:T(128)S(1)}, u32[]{:S(2)}) copy-start(f32[128]{0:T(128)S(1)} %get-tuple-element.253) | copy-start | bytes 1540
  171.7 41.4 %copy-start.115 = (f32[128]{0:T(128)}, f32[128]{0:T(128)S(1)}, u32[]{:S(2)}) copy-start(f32[128]{0:T(128)S(1)} %get-tuple-element.239) | copy-start | bytes 1540
  171.7 365.3 %copy-start.111 = (f32[128]{0:T(128)}, f32[128]{0:T(128)S(1)}, u32[]{:S(2)}) copy-start(f32[128]{0:T(128)S(1)} %get-tuple-element.254) | copy-start | bytes 1540
  235.2 41.5 %all-to-all-start.4 = ((bf16[64,32,384]{2,1,0:T(8,128)(2,1)}), bf16[64,32,384]{2,1,0:T(8,128)(2,1)}, u32[]{:S(2)}, u32[]{:S(2)}) async-start(bf16[64,32,384]{2,1,0:T(8,128)(2,1)} %copy.580), calls=%async_computation.4 | async-start | bytes 3145728 | tf_op jit(solution)/shard_map/all_to_all | solution.py:46
  276.6 40.8 %all-to-all-start.3 = ((bf16[64,32,384]{2,1,0:T(8,128)(2,1)}), bf16[64,32,384]{2,1,0:T(8,128)(2,1)S(1)}, u32[]{:S(2)}, u32[]{:S(2)}) async-start(bf16[64,32,384]{2,1,0:T(8,128)(2,1)} %copy.572), calls=%async_computation.3 | async-start | bytes 3145728 | tf_op jit(solution)/shard_map/all_to_all | solution.py:46
  353.2 41.2 %all-to-all-start.5 = ((bf16[8,8,32,384]{3,2,1,0:T(8,128)(2,1)}), bf16[8,8,32,384]{3,2,1,0:T(8,128)(2,1)}, u32[]{:S(2)}, u32[]{:S(2)}) async-start(bf16[8,8,32,384]{3,2,1,0:T(8,128)(2,1)} %constant_dynamic-update-slice_fusion.8), calls=%async_computation.5 | async-start | bytes 3145728 | tf_op jit(solution)/shard_map/all_to_all | solution.py:52
  399.7 137.4 %copy-start.75 = (f32[32,256]{1,0:T(8,128)}, f32[32,256]{1,0:T(8,128)S(1)}, u32[]{:S(2)}) copy-start(f32[32,256]{1,0:T(8,128)S(1)} %add_rsqrt_fusion) | copy-start | bytes 98308
  480.5 15.7 %copy-start.83 = (bf16[8,256,128]{1,2,0:T(8,128)(2,1)S(1)}, bf16[8,256,128]{1,2,0:T(8,128)(2,1)}, u32[]{:S(2)}) copy-start(bf16[8,256,128]{1,2,0:T(8,128)(2,1)} %copy-done.82) | copy-start | bytes 1572868
  491.7 40.6 %all-to-all-start.8 = ((bf16[8,8,32,384]{3,2,1,0:T(8,128)(2,1)}), bf16[8,8,32,384]{3,2,1,0:T(8,128)(2,1)}, u32[]{:S(2)}, u32[]{:S(2)}) async-start(bf16[8,8,32,384]{3,2,1,0:T(8,128)(2,1)} %constant_dynamic-update-slice_fusion.24), calls=%async_computation.8 | async-start | bytes 3145728 | tf_op jit(solution)/shard_map/all_to_all | solution.py:52
  517.6 19.5 %copy-start.99 = (bf16[1,2,128,128]{3,2,1,0:T(8,128)(2,1)S(1)}, bf16[1,2,128,128]{3,2,1,0:T(8,128)(2,1)}, u32[]{:S(2)}) copy-start(bf16[1,2,128,128]{3,2,1,0:T(8,128)(2,1)} %param.15) | copy-start | bytes 196612
  517.6 19.6 %copy-start.122 = (f32[128]{0:T(128)S(1)}, f32[128]{0:T(128)}, u32[]{:S(2)}) copy-start(f32[128]{0:T(128)} %get-tuple-element.238) | copy-start | bytes 1540
  532.4 40.9 %all-to-all-start.7 = ((bf16[8,8,32,384]{3,2,1,0:T(8,128)(2,1)}), bf16[8,8,32,384]{3,2,1,0:T(8,128)(2,1)}, u32[]{:S(2)}, u32[]{:S(2)}) async-start(bf16[8,8,32,384]{3,2,1,0:T(8,128)(2,1)} %constant_dynamic-update-slice_fusion.16), calls=%async_computation.7 | async-start | bytes 3145728 | tf_op jit(solution)/shard_map/all_to_all | solution.py:52
  643.2 41.1 %all-to-all-start.9 = ((bf16[64,32,384]{2,1,0:T(8,128)(2,1)}), bf16[64,32,384]{2,1,0:T(8,128)(2,1)}, u32[]{:S(2)}, u32[]{:S(2)}) async-start(bf16[64,32,384]{2,1,0:T(8,128)(2,1)} %copy.647), calls=%async_computation.9 | async-start | bytes 3145728 | tf_op jit(solution)/shard_map/all_to_all | solution.py:46
  684.3 36.1 %all-to-all-start.13 = ((bf16[8,16,896]{2,1,0:T(8,128)(2,1)}), bf16[8,16,896]{2,1,0:T(8,128)(2,1)S(1)}, u32[]{:S(2)}, u32[]{:S(2)}) async-start(bf16[8,16,896]{2,1,0:T(8,128)(2,1)} %pad_maximum_fusion.23), calls=%async_computation.13 | async-start | bytes 458752 | tf_op jit(solution)/shard_map/all_to_all | solution.py:68
  720.4 43.1 %all-to-all-start.11 = ((bf16[8,8,32,384]{3,2,1,0:T(8,128)(2,1)}), bf16[8,8,32,384]{3,2,1,0:T(8,128)(2,1)}, u32[]{:S(2)}, u32[]{:S(2)}) async-start(bf16[8,8,32,384]{3,2,1,0:T(8,128)(2,1)} %constant_dynamic-update-slice_fusion.40), calls=%async_computation.11 | async-start | bytes 3145728 | tf_op jit(solution)/shard_map/all_to_all | solution.py:52
  745.0 22.8 %copy-start.3 = (bf16[1,32,256,128]{2,3,1,0:T(8,128)(2,1)S(1)}, bf16[1,32,256,128]{2,3,1,0:T(8,128)(2,1)}, u32[]{:S(2)}) copy-start(bf16[1,32,256,128]{2,3,1,0:T(8,128)(2,1)} %copy-done.2) | copy-start | bytes 6291460
  745.0 22.8 %copy-start.55 = (f32[32,256]{1,0:T(8,128)S(1)}, f32[32,256]{1,0:T(8,128)}, u32[]{:S(2)}) copy-start(f32[32,256]{1,0:T(8,128)} %copy-done.54) | copy-start | bytes 98308
  745.0 22.8 %copy-start.59 = (f32[32,256]{1,0:T(8,128)S(1)}, f32[32,256]{1,0:T(8,128)}, u32[]{:S(2)}) copy-start(f32[32,256]{1,0:T(8,128)} %copy-done.58) | copy-start | bytes 98308
  745.0 22.8 %copy-start.108 = (f32[128]{0:T(128)S(1)}, f32[128]{0:T(128)}, u32[]{:S(2)}) copy-start(f32[128]{0:T(128)} %copy-done.107) | copy-start | bytes 1540
  745.0 22.8 %copy-start.114 = (f32[128]{0:T(128)S(1)}, f32[128]{0:T(128)}, u32[]{:S(2)}) copy-start(f32[128]{0:T(128)} %copy-done.113) | copy-start | bytes 1540
  763.5 67.7 %all-to-all-start.10 = ((bf16[8,8,32,384]{3,2,1,0:T(8,128)(2,1)}), bf16[8,8,32,384]{3,2,1,0:T(8,128)(2,1)}, u32[]{:S(2)}, u32[]{:S(2)}) async-start(bf16[8,8,32,384]{3,2,1,0:T(8,128)(2,1)} %constant_dynamic-update-slice_fusion.32), calls=%async_computation.10 | async-start | bytes 3145728 | tf_op jit(solution)/shard_map/all_to_all | solution.py:52
  887.2 47.7 %collective-permute-start = (bf16[32,256,128]{1,2,0:T(8,128)(2,1)S(1)}, bf16[32,256,128]{1,2,0:T(8,128)(2,1)}, u32[]{:S(2)}, u32[]{:S(2)}) collective-permute-start(bf16[32,256,128]{1,2,0:T(8,128)(2,1)S(1)} %fusion.64), channel_id=1, source_target_pairs={{0,24},{8,0},{16,8},{24,16},{1,25},{9,1},{17,9},{25,17},{2,26},{10... | collective-permute-start | bytes 6291464 | tf_op jit(solution)/shard_map/ppermute | solution.py:11
  888.2 12.9 %all-to-all-start.12 = ((bf16[8,16,896]{2,1,0:T(8,128)(2,1)}), bf16[8,16,896]{2,1,0:T(8,128)(2,1)S(1)}, u32[]{:S(2)}, u32[]{:S(2)}) async-start(bf16[8,16,896]{2,1,0:T(8,128)(2,1)} %pad_maximum_fusion.22), calls=%async_computation.12 | async-start | bytes 458752 | tf_op jit(solution)/shard_map/all_to_all | solution.py:68
  (110 other events, 552.4 us)
